TPU v7x, 32 devices: a whole 2x2x4 slice. The times are simulated.
32 devices in a mesh: shard: 2 (over x), ex: 8 (over z, y), tp: 2 (over core).
Axes of the slice: x: 2, y: 2, z: 4, core: 2. Of those that a mesh axis runs over, the one named last changes fastest.
Arguments:
- hidden: bfloat16 [4096, 28672], P(('shard', 'ex'), 'tp'), parts along dimension 0, may hold values from -6 to 6
- out_grad: bfloat16 [4096, 8192], P(('shard', 'ex'), 'tp'), parts along dimension 0, may hold values from -6 to 6
- token_live: int32 [4096], P(('shard', 'ex')), parts along dimension 0, may hold values 0 or 1
- proj_in: bfloat16 [28672, 64], P('tp'), may hold values from -0.03125 to 0.03125
- proj_out: bfloat16 [8192, 64], P('tp'), may hold values from -0.0625 to 0.0625
- query_bank: bfloat16 [1024, 4096], P('ex'), may hold values from -0.01171875 to 0.01171875
Outputs:
- scores: float32 [64, 1024], P(('shard', 'ex')), parts along dimension 0
There are 2 independent parts, one for each index of `shard`. A program takes and returns all parts, laid end to end along the dimension named above; an argument that names none is the same for every part. Nothing has to cross between parts.
All inputs are finite; a program needn't handle non-finite values. No bound on the sum of `token_live` on one device may be relied on, other than what follows from the above.
Results may differ from a plain program's by a relative error of at most 0.0029.
Values may be sent and summed in bfloat16 or wider, within the bound.
A program may use at most 64 MiB of HBM per device.

v0:
```python
import jax
import jax.numpy as jnp
from jax import lax
from jax.sharding import PartitionSpec as P

R1 = 64
R2 = 64
SEQ = 64


def local(hidden, out_grad, token_live, proj_in, proj_out, query_bank):
    in_part = jnp.dot(hidden, proj_in, preferred_element_type=jnp.float32)
    out_part = jnp.dot(out_grad, proj_out, preferred_element_type=jnp.float32)
    in_proj, out_proj = lax.psum((in_part, out_part), "tp")
    in_proj = in_proj * token_live.astype(jnp.float32)[:, None]
    ex_local = hidden.shape[0] // SEQ
    left = in_proj.reshape(ex_local, SEQ, R1)
    right = out_proj.reshape(ex_local, SEQ, R2)
    grads = jnp.einsum("eti,etj->eij", left, right, precision=lax.Precision.HIGHEST)
    grads = grads.reshape(ex_local, R1 * R2).astype(jnp.bfloat16)
    return lax.dot_general(
        grads,
        lax.all_gather(query_bank, "ex", axis=0, tiled=True),
        (((1,), (1,)), ((), ())),
        preferred_element_type=jnp.float32,
    )


def solution(mesh):
    placed = (
        P(("shard", "ex"), "tp"),
        P(("shard", "ex"), "tp"),
        P(("shard", "ex")),
        P("tp", None),
        P("tp", None),
        P("ex", None),
    )
    return jax.shard_map(
        local, mesh=mesh, in_specs=placed, out_specs=P(("shard", "ex"), None), check_vma=False
    )
```

profile of v0, /device:TPU:0, one launch (start us, length us, event | category | flops | bytes accessed | tf_op | source)
XLA Modules:
  0.0 161.5 jit_solution(16098245214789247294)
XLA Ops:
  7.4 0.0 copy-start
  7.4 0.0 copy-start.1
  7.4 0.0 all-reduce.3.cloned.1.call-start
  7.4 1.6 copy-done
  9.0 2.4 %fusion.2 = f32[256,64]{1,0:T(8,128)} fusion(bf16[256,4096]{1,0:T(8,128)(2,1)S(1)} %copy-done, bf16[4096,64]{0,1:T(8,128)(2,1)} %param.10), kind=kOutput, calls=%fused_computation.4 | convolution fusion | flops 134217728 | bytes 2686976 | tf_op jit(solution)/shard_map/reshape | solution.py:18
  11.3 6.6 %fusion.1 = f32[256,64]{0,1:T(8,128)} fusion(bf16[256,14336]{1,0:T(8,128)(2,1)} %param.6, bf16[14336,64]{0,1:T(8,128)(2,1)} %param.9), kind=kOutput, calls=%fused_computation.3 | convolution fusion | flops 469762048 | bytes 9240576 | tf_op jit(solution)/shard_map/dot_general | solution.py:12
  17.9 0.0 all-reduce.3.cloned.1.call-update
  17.9 0.0 all-gather.2.cloned.1.call-start
  18.0 0.5 all-gather.2.cloned.1.call-update
  18.5 0.0 copy-done.1
  18.5 20.4 %all-reduce.3.cloned.1.call-done = (f32[4,64,64]{2,1,0:T(8,128)}, f32[256,64]{0,1:T(8,128)}) async-done(((f32[4,64,64]{2,1,0:T(8,128)}, f32[256,64]{0,1:T(8,128)}), (f32[4,64,64]{2,1,0:T(8,128)}, f32[256,64]{0,1:T(8,128)})) %all-reduce.3.cloned.1.call-update) | async-done | bytes 131088 | tf_op jit(solution)/shard_map/psum | solution.py:14
  38.9 0.8 broadcast_multiply_fusion
  39.8 0.1 reshape.9
  39.9 1.2 convolution_convert_fusion
  41.0 0.1 convert_element_type.11
  41.2 106.6 %all-gather.2.cloned.1.call-done = bf16[1024,4096]{1,0:T(8,128)(2,1)} async-done(((bf16[128,4096]{1,0:T(8,128)(2,1)}), bf16[1024,4096]{1,0:T(8,128)(2,1)}) %all-gather.2.cloned.1.call-update) | async-done | bytes 8388624 | tf_op jit(solution)/shard_map/all_gather | solution.py:23
  147.8 6.3 %fusion.3 = f32[4,1024]{1,0:T(4,128)} fusion(bf16[4,4096]{1,0:T(4,128)(2,1)S(1)} %convert_element_type.11, bf16[1024,4096]{1,0:T(8,128)(2,1)} %all-gather.2.cloned.1.call-done), kind=kOutput, calls=%fused_computation.5 | convolution fusion | flops 33554432 | bytes 8437760 | tf_op jit(solution)/shard_map/dot_general | solution.py:21
  (1 shorter events, 0.0 us)
Async XLA Ops:
  7.4 1.6 copy-start
  7.4 11.1 %copy-start.1 = (s32[256]{0:T(256)S(1)}, s32[256]{0:T(256)}, u32[]{:S(2)}) copy-start(s32[256]{0:T(256)} %param.8) | copy-start | bytes 3076
  7.4 31.5 %all-reduce.3.cloned.1.call-start = ((), (), s32[]{:S(2)}) async-start(), calls=%async_computation.1 | async-start | bytes 393216 | tf_op jit(solution)/shard_map/psum | solution.py:14
  17.9 129.8 %all-gather.2.cloned.1.call-start = ((), (), s32[]{:S(2)}) async-start(), calls=%async_computation | async-start | bytes 9437184 | tf_op jit(solution)/shard_map/all_gather | solution.py:23
Sparse Core Ops, SparseCore 0:
  18.0 20.8 all-reduce.2
Sparse Core Ops, SparseCore 1:
  20.5 127.2 all-gather.1
where the time goes:
time: 162 us; the launch traced here: 161 us
  waiting for transfers between devices  128 us (79%)
  matrix products  16.4 us (10%)
  between operations  14.9 us (9%)
  local copies, waits for them, and re-layouts  1.82 us (1%)
    all_gather x1, waiting for transfers between devices, local(): lax.all_gather(query_bank, 'ex', axis=0, tiled=True)  107 us
    psum x1, waiting for transfers between devices, local(): in_proj, out_proj = lax.psum((in_part, out_part), 'tp')  20.4 us
    dot_general x1, matrix products, local(): in_part = jnp.dot(hidden, proj_in, preferred_element_type=jnp.float32)  6.56 us
    dot_general x1, matrix products, local(): lax.dot_general(grads, lax.all_gather(query_bank, 'ex', axis=0, tiled=Tru...  6.26 us
  transfers between devices with their start and end apart: 2, of which 2 were waited for; matrix products, arithmetic and copies ran while one was open for 1% of the time, Pallas kernels for 0%

commit v1 on v0

v1 whole, which is shorter than its diff:
```python
import functools

import jax
import jax.numpy as jnp
from jax import lax
from jax.experimental import pallas as pl
from jax.experimental.pallas import tpu as pltpu
from jax.sharding import PartitionSpec as P

R1 = 64
R2 = 64
SEQ = 64
LANES = 128
CHUNKS = 4
MESH = pl.DeviceIdType.MESH
NT = (((1,), (1,)), ((), ()))


def each(n, body):
    if n <= 16:
        for i in range(n):
            body(i)
    else:
        lax.fori_loop(0, n, lambda i, _: (body(i), 0)[1], 0)


def kernel(
    n_ex, hid_hbm, og_hbm, live_hbm, pin_hbm, pout_hbm, qb_hbm, res_hbm,
    hid, og, live, pin, pout, qb, msg_out, msg_in, in_t, grads, wide, sbuf,
    hid_sem, pin_sem, og_sem, small_sem, tp_sem, g_send, g_recv, s_send, s_recv, own_sem,
):
    shard, ex, tp = lax.axis_index("shard"), lax.axis_index("ex"), lax.axis_index("tp")
    half = hid_hbm.shape[0] // 2
    own_ex = half // SEQ
    block = own_ex * R1 * R2 // LANES
    pairs = R1 * R2 // LANES
    rows = (pl.ds(pl.multiple_of((1 - tp) * half, half), half), pl.ds(pl.multiple_of(tp * half, half), half))
    width = hid_hbm.shape[1] // CHUNKS

    loads = {}

    def load(name, src, dst, sem):
        loads[name] = pltpu.make_async_copy(src, dst, sem)
        loads[name].start()

    load("pout", pout_hbm, pout, small_sem.at[0])
    load(("og", 0), og_hbm.at[rows[0]], og.at[0], og_sem.at[0])
    for c in range(CHUNKS):
        cols = pl.ds(c * width, width)
        load(("pin", c), pin_hbm.at[:, cols], pin.at[:, cols], pin_sem.at[c])
        load(("hid", 0, c), hid_hbm.at[rows[0], cols], hid.at[0, :, cols], hid_sem.at[0, c])
    load(("og", 1), og_hbm.at[rows[1]], og.at[1], og_sem.at[1])
    load("live", live_hbm.at[:, rows[1]], live, small_sem.at[1])
    for c in range(CHUNKS):
        cols = pl.ds(c * width, width)
        load(("hid", 1, c), hid_hbm.at[rows[1], cols], hid.at[1, :, cols], hid_sem.at[1, c])
    load("qb", qb_hbm, qb, small_sem.at[2])

    barrier = pltpu.get_barrier_semaphore()

    def greet(s):
        pl.semaphore_signal(
            barrier, inc=1, device_id=(shard, lax.rem(ex + s // 2, n_ex), lax.rem(tp + s % 2, 2)), device_id_type=MESH
        )

    each(2 * n_ex - 1, lambda s: greet(s + 1))

    def project(h):
        loads["og", h].wait()
        if h == 0:
            loads["pout"].wait()
        right = lax.dot_general(og[h], pout[...], NT, preferred_element_type=jnp.float32)
        left = jnp.zeros((half, R1), jnp.float32)
        for c in range(CHUNKS):
            cols = pl.ds(c * width, width)
            if h == 0:
                loads["pin", c].wait()
            loads["hid", h, c].wait()
            left += lax.dot_general(hid[h, :, cols], pin[:, cols], NT, preferred_element_type=jnp.float32)
        return jnp.concatenate([left, right], axis=1)

    msg_out[...] = project(0)
    pl.semaphore_wait(barrier, 2 * n_ex - 1)
    swap = pltpu.make_async_remote_copy(
        src_ref=msg_out, dst_ref=msg_in, send_sem=tp_sem.at[0], recv_sem=tp_sem.at[1],
        device_id=(shard, ex, 1 - tp), device_id_type=MESH,
    )
    swap.start()
    mine = project(1)
    swap.wait_recv()
    both = mine + msg_in[...]

    in_t[...] = both.T[:R1]
    even = in_t[pl.ds(0, R1 // 2, stride=2), :]
    odd = in_t[pl.ds(1, R1 // 2, stride=2), :]
    loads["live"].wait()
    alive = live[...].astype(jnp.float32)
    token = lax.broadcasted_iota(jnp.int32, (1, half), 1)
    lefts = []
    for e in range(own_ex):
        keep = jnp.where((token >= e * SEQ) & (token < (e + 1) * SEQ), alive, 0.0)
        lefts.append(jnp.concatenate([even * keep, odd * keep], axis=1))
    low = lax.broadcasted_iota(jnp.int32, (half, LANES), 1) < R2
    turned = pltpu.roll(both, R2, 1)
    right = jnp.concatenate([jnp.where(low, turned, 0.0), jnp.where(low, 0.0, both)], axis=0)
    grad = jnp.dot(
        jnp.concatenate(lefts, axis=0), right, precision=lax.Precision.HIGHEST, preferred_element_type=jnp.float32
    )
    slot = grads.at[pl.ds(pl.multiple_of(ex * block, block), block)]
    slot[...] = grad.astype(jnp.bfloat16)

    def grad_copy(peer, owner):
        where = grads.at[pl.ds(pl.multiple_of(owner * block, block), block)]
        return pltpu.make_async_remote_copy(
            src_ref=where, dst_ref=where, send_sem=g_send.at[peer], recv_sem=g_recv.at[owner],
            device_id=(shard, peer, tp), device_id_type=MESH,
        )

    def around(s):
        return lax.rem(ex + s, n_ex)

    each(n_ex - 1, lambda s: grad_copy(around(s + 1), ex).start())
    each(n_ex - 1, lambda s: grad_copy(around(s + 1), around(s + 1)).wait_recv())

    wide[...] = grads[...].astype(jnp.float32)
    flat = jnp.concatenate(
        [wide[pl.ds(k, n_ex * own_ex, stride=pairs), :].astype(jnp.bfloat16) for k in range(pairs)], axis=1
    )
    loads["qb"].wait()
    scores = lax.dot_general(flat, qb[...], NT, preferred_element_type=jnp.float32)
    for j in range(n_ex):
        sbuf[j] = scores[j * own_ex : (j + 1) * own_ex]

    def score_copy(peer, core, owner, owner_core):
        return pltpu.make_async_remote_copy(
            src_ref=sbuf.at[peer], dst_ref=res_hbm.at[owner, owner_core],
            send_sem=s_send.at[core, peer], recv_sem=s_recv.at[owner_core, owner],
            device_id=(shard, peer, core), device_id_type=MESH,
        )

    def partner(s):
        return around(s // 2), lax.rem(tp + s % 2, 2)

    each(2 * n_ex - 1, lambda s: score_copy(*partner(s + 1), ex, tp).start())
    keep_own = pltpu.make_async_copy(sbuf.at[ex], res_hbm.at[ex, tp], own_sem)
    keep_own.start()
    swap.wait_send()
    each(n_ex - 1, lambda s: grad_copy(around(s + 1), ex).wait_send())
    each(2 * n_ex - 1, lambda s: score_copy(*partner(s + 1), *partner(s + 1)).wait_recv())
    each(2 * n_ex - 1, lambda s: score_copy(*partner(s + 1), ex, tp).wait_send())
    keep_own.wait()


def local(n_ex, hidden, out_grad, token_live, proj_in, proj_out, query_bank):
    tokens, hid_width = hidden.shape
    half, own_ex = tokens // 2, tokens // 2 // SEQ
    queries = query_bank.shape[0]
    block = own_ex * R1 * R2 // LANES
    hbm = pl.BlockSpec(memory_space=pl.ANY)
    dma = pltpu.SemaphoreType.DMA
    result = pl.pallas_call(
        functools.partial(kernel, n_ex),
        out_shape=jax.ShapeDtypeStruct((n_ex, 2, own_ex, queries), jnp.float32),
        in_specs=[hbm] * 6,
        out_specs=hbm,
        scratch_shapes=[
            pltpu.VMEM((2, half, hid_width), jnp.bfloat16),
            pltpu.VMEM((2, half, out_grad.shape[1]), jnp.bfloat16),
            pltpu.VMEM((1, half), jnp.int32),
            pltpu.VMEM((R1, hid_width), jnp.bfloat16),
            pltpu.VMEM((R2, out_grad.shape[1]), jnp.bfloat16),
            pltpu.VMEM(query_bank.shape, jnp.bfloat16),
            pltpu.VMEM((half, R1 + R2), jnp.float32),
            pltpu.VMEM((half, R1 + R2), jnp.float32),
            pltpu.VMEM((R1, half), jnp.float32),
            pltpu.VMEM((n_ex * block, LANES), jnp.bfloat16),
            pltpu.VMEM((n_ex * block, LANES), jnp.float32),
            pltpu.VMEM((n_ex, own_ex, queries), jnp.float32),
            dma((2, CHUNKS)), dma((CHUNKS,)), dma((2,)), dma((3,)), dma((2,)),
            dma((n_ex,)), dma((n_ex,)), dma((2, n_ex)), dma((2, n_ex)), dma,
        ],
        compiler_params=pltpu.CompilerParams(
            collective_id=0, has_side_effects=True, vmem_limit_bytes=56 * 1024 * 1024
        ),
        name="attribute",
    )(hidden, out_grad, token_live.reshape(1, tokens), proj_in.T, proj_out.T, query_bank)
    return result.reshape(n_ex, 2 * own_ex, queries).transpose(1, 0, 2).reshape(2 * own_ex, n_ex * queries)


def solution(mesh):
    placed = (
        P(("shard", "ex"), "tp"),
        P(("shard", "ex"), "tp"),
        P(("shard", "ex")),
        P("tp", None),
        P("tp", None),
        P("ex", None),
    )
    return jax.shard_map(
        functools.partial(local, mesh.shape["ex"]),
        mesh=mesh, in_specs=placed, out_specs=P(("shard", "ex"), None), check_vma=False,
    )
```

time: 162 us -> 23.6 us (0.15)
  waiting for transfers between devices: 128 us -> 0 us
  Pallas kernels: 0 us -> 22.1 us
  matrix products: 16.4 us -> 0 us
  between operations: 14.9 us -> 0.01 us
    all_gather x1 -> x0, waiting for transfers between devices: 107 us -> none  [local(): lax.all_gather(query_bank, 'ex', axis=0, tiled=True)]
    pallas_call x0 -> x1, Pallas kernels: none -> 22.1 us  [local(): pl.pallas_call(functools.partial(kernel, n_ex), out_shape=jax.ShapeDtypeS...]
    psum x1 -> x0, waiting for transfers between devices: 20.4 us -> none  [local(): in_proj, out_proj = lax.psum((in_part, out_part), 'tp')]
    dot_general x3 -> x0, matrix products: 14 us -> none  [the longest x1 6.56 us: local(): in_part = jnp.dot(hidden, proj_in, preferred_element_type=jnp.float32)]
    reshape x1 -> x0, matrix products: 2.38 us -> none  [local(): right = out_proj.reshape(ex_local, SEQ, R2)]
  transfers between devices with their start and end apart: 2 -> 0, of which waited for: 2 -> 0; matrix products, arithmetic and copies ran while one was open for 1% -> 0% of each run, Pallas kernels for 0% -> 0%
where the time goes in v1:
time: 23.6 us; the launch traced here: 23.4 us
  Pallas kernels  22.1 us (94%)
  local copies, waits for them, and re-layouts  1.32 us (6%)
    pallas_call x1, Pallas kernels, local(): pl.pallas_call(functools.partial(kernel, n_ex), out_shape=jax.ShapeDtypeS...  22.1 us
    unnamed x1, local copies, waits for them, and re-layouts  1.32 us

profile of v1, /device:TPU:0, one launch (start us, length us, event | category | flops | bytes accessed | tf_op | source)
XLA Modules:
  0.0 23.4 jit_solution(13847891787829108134)
XLA Ops:
  0.0 22.1 %attribute.1 = f32[8,2,2,128]{3,2,1,0:T(2,128)} custom-call(bf16[256,14336]{1,0:T(8,128)(2,1)} %hid_hbm.1, bf16[256,4096]{1,0:T(8,128)(2,1)} %og_hbm.1, s32[1,256]{1,0:T(1,128)} %bitcast.11, bf16[64,14336]{1,0:T(8,128)(2,1)} %bitcast.8, bf16[64,4096]{1,0:T(8,128)(2,1)} %bitcast.9, bf16[128,4096]{1,0:T(8,128)(2,1)} %qb_hbm.1), custom_call_target="tpu_custom_call" | custom-call | tf_op jit(solution)/shard_map/attribute/pallas_call | solution.py:161
  22.1 1.3 %copy.9 = f32[4,1024]{1,0:T(4,128)} copy(f32[4,1024]{1,0:T(4,128)} %bitcast.10) | data formatting | bytes 32768

commit v2 on v1

v2 whole, which is shorter than its diff:
```python
import functools

import jax
import jax.numpy as jnp
from jax import lax
from jax.experimental import pallas as pl
from jax.experimental.pallas import tpu as pltpu
from jax.sharding import PartitionSpec as P

R1 = 64
R2 = 64
SEQ = 64
LANES = 128
MESH = pl.DeviceIdType.MESH
NT = (((1,), (1,)), ((), ()))


def each(n, body):
    if n <= 16:
        for i in range(n):
            body(i)
    else:
        lax.fori_loop(0, n, lambda i, _: (body(i), 0)[1], 0)


def kernel(
    n_ex, hid_hbm, og_hbm, live_hbm, pin_hbm, pout_hbm, qb_hbm, res,
    hid, og, live, pin, pout, qb, msg_out, msg_in, in_t, grads, wide, sbuf,
    hid_sem, og_sem, small_sem, tp_sem, g_send, g_recv, s_send, s_recv,
):
    shard, ex, tp = lax.axis_index("shard"), lax.axis_index("ex"), lax.axis_index("tp")
    half = hid_hbm.shape[0] // 2
    own_ex = half // SEQ
    pairs = R1 * R2 // LANES
    theirs, ours = pl.multiple_of((1 - tp) * half, half), pl.multiple_of(tp * half, half)

    def load(src, dst, sem):
        copy = pltpu.make_async_copy(src, dst, sem)
        copy.start()
        return copy

    get_pout = load(pout_hbm, pout, small_sem.at[0])
    get_og = [load(og_hbm.at[pl.ds(theirs, half)], og.at[pl.ds(0, half)], og_sem.at[0])]
    get_pin = load(pin_hbm, pin, small_sem.at[1])
    get_first = load(hid_hbm.at[pl.ds(theirs, half)], hid.at[pl.ds(0, half)], hid_sem.at[0])
    get_og.append(load(og_hbm.at[pl.ds(ours, half)], og.at[pl.ds(half, half)], og_sem.at[1]))
    get_live = load(live_hbm.at[:, pl.ds(ours, half)], live, small_sem.at[2])
    get_second = load(hid_hbm.at[pl.ds(ours, half)], hid.at[pl.ds(half, half)], hid_sem.at[1])
    get_qb = load(qb_hbm, qb, small_sem.at[3])

    def around(s):
        return jnp.where(ex + s >= n_ex, ex + s - n_ex, ex + s)

    def partner(s):
        return around(s // 2), (tp if s % 2 == 0 else 1 - tp) if isinstance(s, int) else lax.rem(tp + s % 2, 2)

    barrier = pltpu.get_barrier_semaphore()

    def greet(s):
        pl.semaphore_signal(barrier, inc=1, device_id=(shard, *partner(s)), device_id_type=MESH)

    each(2 * n_ex - 1, lambda s: greet(s + 1))

    get_pout.wait()
    get_og[0].wait()
    msg_out[R1:] = lax.dot_general(pout[...], og[:half], NT, preferred_element_type=jnp.float32)
    get_pin.wait()
    get_first.wait()
    msg_out[:R1] = lax.dot_general(pin[...], hid[:half], NT, preferred_element_type=jnp.float32)
    pl.semaphore_wait(barrier, 2 * n_ex - 1)
    swap = pltpu.make_async_remote_copy(
        src_ref=msg_out, dst_ref=msg_in, send_sem=tp_sem.at[0], recv_sem=tp_sem.at[1],
        device_id=(shard, ex, 1 - tp), device_id_type=MESH,
    )
    swap.start()

    def grad_copy(peer, owner):
        block = own_ex * pairs
        where = grads.at[pl.ds(pl.multiple_of(owner * block, block), block)]
        return pltpu.make_async_remote_copy(
            src_ref=where, dst_ref=where, send_sem=g_send.at[peer], recv_sem=g_recv.at[owner],
            device_id=(shard, peer, tp), device_id_type=MESH,
        )

    get_og[1].wait()
    right = lax.dot_general(pout[...], og[half:], NT, preferred_element_type=jnp.float32)
    get_live.wait()
    get_second.wait()
    left = lax.dot_general(pin[...], hid[half:], NT, preferred_element_type=jnp.float32)
    swap.wait_recv()
    in_half = (left + msg_in[:R1]) * live[...].astype(jnp.float32)
    out_t = right + msg_in[R1:]

    in_t[...] = in_half
    even = in_t[pl.ds(0, R1 // 2, stride=2), :]
    odd = in_t[pl.ds(1, R1 // 2, stride=2), :]
    token = lax.broadcasted_iota(jnp.int32, (1, half), 1)
    lefts = []
    for e in range(own_ex):
        mine = (token >= e * SEQ) & (token < (e + 1) * SEQ)
        lefts.append(jnp.concatenate([jnp.where(mine, even, 0.0), jnp.where(mine, odd, 0.0)], axis=1))
    none = jnp.zeros_like(out_t)
    both = jnp.concatenate(
        [jnp.concatenate([out_t, none], axis=1), jnp.concatenate([none, out_t], axis=1)], axis=0
    )
    grad = lax.dot_general(
        jnp.concatenate(lefts, axis=0), both, NT,
        precision=lax.Precision.HIGHEST, preferred_element_type=jnp.float32,
    )
    block = own_ex * pairs
    grads[pl.ds(pl.multiple_of(ex * block, block), block)] = grad.astype(jnp.bfloat16)
    each(n_ex - 1, lambda s: grad_copy(around(s + 1), ex).start())
    each(n_ex - 1, lambda s: grad_copy(around(s + 1), around(s + 1)).wait_recv())

    wide[...] = grads[...].astype(jnp.float32)
    flat = jnp.concatenate(
        [wide[pl.ds(k, n_ex * own_ex, stride=pairs), :].astype(jnp.bfloat16) for k in range(pairs)], axis=1
    )
    get_qb.wait()
    scores = lax.dot_general(flat, qb[...], NT, preferred_element_type=jnp.float32)
    for j in range(n_ex):
        sbuf[j] = scores[j * own_ex : (j + 1) * own_ex]

    def score_copy(peer, core, owner, owner_core):
        return pltpu.make_async_remote_copy(
            src_ref=sbuf.at[peer], dst_ref=res.at[owner, owner_core],
            send_sem=s_send.at[core, peer], recv_sem=s_recv.at[owner_core, owner],
            device_id=(shard, peer, core), device_id_type=MESH,
        )

    each(2 * n_ex - 1, lambda s: score_copy(*partner(s + 1), ex, tp).start())
    res[ex, tp] = sbuf[ex]
    swap.wait_send()
    each(n_ex - 1, lambda s: grad_copy(around(s + 1), ex).wait_send())
    each(2 * n_ex - 1, lambda s: score_copy(*partner(s + 1), *partner(s + 1)).wait_recv())
    each(2 * n_ex - 1, lambda s: score_copy(*partner(s + 1), ex, tp).wait_send())


def local(n_ex, hidden, out_grad, token_live, proj_in, proj_out, query_bank):
    tokens, hid_width = hidden.shape
    half, own_ex = tokens // 2, tokens // 2 // SEQ
    queries = query_bank.shape[0]
    block = own_ex * R1 * R2 // LANES
    hbm = pl.BlockSpec(memory_space=pl.ANY)
    dma = pltpu.SemaphoreType.DMA
    result = pl.pallas_call(
        functools.partial(kernel, n_ex),
        out_shape=pltpu.VMEM((n_ex, 2, own_ex, queries), jnp.float32),
        in_specs=[hbm] * 6,
        out_specs=pl.BlockSpec(memory_space=pltpu.VMEM),
        scratch_shapes=[
            pltpu.VMEM((tokens, hid_width), jnp.bfloat16),
            pltpu.VMEM(out_grad.shape, jnp.bfloat16),
            pltpu.VMEM((1, half), jnp.int32),
            pltpu.VMEM((R1, hid_width), jnp.bfloat16),
            pltpu.VMEM((R2, out_grad.shape[1]), jnp.bfloat16),
            pltpu.VMEM(query_bank.shape, jnp.bfloat16),
            pltpu.VMEM((R1 + R2, half), jnp.float32),
            pltpu.VMEM((R1 + R2, half), jnp.float32),
            pltpu.VMEM((R1, half), jnp.float32),
            pltpu.VMEM((n_ex * block, LANES), jnp.bfloat16),
            pltpu.VMEM((n_ex * block, LANES), jnp.float32),
            pltpu.VMEM((n_ex, own_ex, queries), jnp.float32),
            dma((2,)), dma((2,)), dma((4,)), dma((2,)),
            dma((n_ex,)), dma((n_ex,)), dma((2, n_ex)), dma((2, n_ex)),
        ],
        compiler_params=pltpu.CompilerParams(
            collective_id=0, has_side_effects=True, vmem_limit_bytes=56 * 1024 * 1024
        ),
        name="attribute",
    )(hidden, out_grad, token_live.reshape(1, tokens), proj_in.T, proj_out.T, query_bank)
    return result.reshape(n_ex, 2 * own_ex, queries).transpose(1, 0, 2).reshape(2 * own_ex, n_ex * queries)


def solution(mesh):
    placed = (
        P(("shard", "ex"), "tp"),
        P(("shard", "ex"), "tp"),
        P(("shard", "ex")),
        P("tp", None),
        P("tp", None),
        P("ex", None),
    )
    return jax.shard_map(
        functools.partial(local, mesh.shape["ex"]),
        mesh=mesh, in_specs=placed, out_specs=P(("shard", "ex"), None), check_vma=False,
    )
```

time: 23.6 us -> 22.3 us (0.945)
  local copies, waits for them, and re-layouts: 1.32 us -> 0.61 us
  Pallas kernels: 22.1 us -> 21.6 us
    unnamed x1, local copies, waits for them, and re-layouts: 1.32 us -> 0.61 us
    pallas_call x1, Pallas kernels: 22.1 us -> 21.6 us  [local(): pl.pallas_call(functools.partial(kernel, n_ex), out_shape=pltpu.VMEM((n_e...]
where the time goes in v2:
time: 22.3 us; the launch traced here: 22.2 us
  Pallas kernels  21.6 us (97%)
  local copies, waits for them, and re-layouts  0.61 us (3%)
    pallas_call x1, Pallas kernels, local(): pl.pallas_call(functools.partial(kernel, n_ex), out_shape=pltpu.VMEM((n_e...  21.6 us
    unnamed x1, local copies, waits for them, and re-layouts  0.61 us

profile of v2, /device:TPU:0, one launch (start us, length us, event | category | flops | bytes accessed | tf_op | source)
XLA Modules:
  0.0 22.2 jit_solution(7194421928278797086)
XLA Ops:
  0.0 21.6 %attribute.1 = f32[8,2,2,128]{3,2,1,0:T(2,128)S(1)} custom-call(bf16[256,14336]{1,0:T(8,128)(2,1)} %hid_hbm.1, bf16[256,4096]{1,0:T(8,128)(2,1)} %og_hbm.1, s32[1,256]{1,0:T(1,128)} %bitcast.11, bf16[64,14336]{1,0:T(8,128)(2,1)} %bitcast.9, bf16[64,4096]{1,0:T(8,128)(2,1)} %bitcast.10, bf16[128,4096]{1,0:T(8,128)(2,1)} %qb_hbm.1), custom_call_target="tpu_custom_call" | custom-call | tf_op jit(solution)/shard_map/attribute/pallas_call | solution.py:146
  21.6 0.6 %copy.9 = f32[4,1024]{1,0:T(4,128)} copy(f32[4,1024]{1,0:T(4,128)S(1)} %bitcast.8) | data formatting | bytes 32768
